TPU v7x, 128 devices: a whole 4x4x4 slice. The times are simulated.
128 devices in a mesh: wide: 16 (over z, x), narrow: 8 (over y, core).
Axes of the slice: x: 4, y: 4, z: 4, core: 2. Of those that a mesh axis runs over, the one named last changes fastest.
Arguments:
- cotangent: float32 [1536, 256, 256], P(('wide', 'narrow')), may hold values from -6 to 6
- row_basis: float32 [1536, 256, 128], P(('wide', 'narrow')), may hold values from -0.375 to 0.375
- col_basis: float32 [1536, 256, 128], P(('wide', 'narrow')), may hold values from -0.5 to 0.5
- leaf_up: float32 [1536, 128, 128], P(('wide', 'narrow')), may hold values from -0.15625 to 0.15625
- node_up: float32 [128, 128, 128], P(('wide', 'narrow')), may hold values from -0.1875 to 0.1875
- node_couple: float32 [128, 2, 128, 128], P(('wide', 'narrow')), may hold values from -0.375 to 0.375
- group_couple: float32 [16, 8, 128, 128], P('wide', 'narrow'), may hold values from -0.1875 to 0.1875
- node_down: float32 [128, 128, 128], P(('wide', 'narrow')), may hold values from -0.5 to 0.5
- leaf_down: float32 [1536, 128, 128], P(('wide', 'narrow')), may hold values from -0.5 to 0.5
- near_blocks: float32 [1536, 4, 256, 256], P(('wide', 'narrow')), may hold values from -0.1875 to 0.1875
- near_index: int32 [1536, 4], P(('wide', 'narrow')), may hold values from 0 to 1535, as said below
- far_nodes: int32 [128, 2], P(('wide', 'narrow')), may hold values from 0 to 7, as said below
- far_groups: int32 [16, 8], P('wide', 'narrow'), may hold values from 0 to 15, as said below
Outputs:
- product: float32 [1536, 256, 256], P(('wide', 'narrow'))
Inputs may be any that keep to these rules, and one draw needn't show every extreme that they name: near_index[l, 0] is l; every other entry differs from l by 1 to 2. far_nodes[d, j] never equals d % 8; the entries of a row differ. far_groups[g, j] never equals g; the entries of a row differ.
All inputs are finite; a program needn't handle non-finite values.
Results may differ from a plain program's by a relative error of at most 0.000062.
Values sent between devices are 32-bit elements; how exact they have to be, the bound alone decides.
A program may use at most 128 MiB of HBM per device.

v0:
```python
import jax
import jax.numpy as jnp
from jax import lax
from jax.sharding import PartitionSpec as P

NEAR_REACH = 2
HIGH = lax.Precision.HIGHEST


def from_behind(value, axis, steps):
    count = lax.axis_size(axis)
    leading, last = (max(0, -steps), min(count, count - steps))
    return lax.ppermute(value, axis, [(source, source + steps) for source in range(leading, last)])


def shards(
    cotangent,
    row_basis,
    col_basis,
    leaf_up,
    node_up,
    node_couple,
    group_couple,
    node_down,
    leaf_down,
    near_blocks,
    near_index,
    far_nodes,
    far_groups,
):
    leaves = cotangent.shape[0]
    lower = from_behind(cotangent[leaves - NEAR_REACH :], ("wide", "narrow"), 1)
    upper = from_behind(cotangent[:NEAR_REACH], ("wide", "narrow"), -1)
    leaf_coeffs = jnp.einsum("lpk,lpv->lkv", row_basis, cotangent, precision=HIGH)
    node_coeffs = jnp.einsum("lkm,lkv->mv", leaf_up, leaf_coeffs, precision=HIGH)
    up_term = jnp.dot(node_up[0].T, node_coeffs, precision=HIGH)
    siblings = lax.all_gather(node_coeffs[None], "narrow", axis=0, tiled=True)
    group_coeffs = lax.psum(up_term, "narrow")
    picked = siblings[far_nodes[0]]
    node_out = jnp.einsum("jkm,jkv->mv", node_couple[0], picked, precision=HIGH)
    all_groups = lax.all_gather(group_coeffs[None], "wide", axis=0, tiled=True)
    picked_groups = all_groups[far_groups[0]]
    partial_value = jnp.einsum("jkm,jkv->mv", group_couple[0], picked_groups, precision=HIGH)
    group_out = lax.psum(partial_value, "narrow")
    node_total = node_out + jnp.dot(node_down[0], group_out, precision=HIGH)
    leaf_total = jnp.einsum("lmk,kv->lmv", leaf_down, node_total, precision=HIGH)
    far_part = jnp.einsum("lpk,lkv->lpv", col_basis, leaf_total, precision=HIGH)
    extended = jnp.concatenate([lower, cotangent, upper], axis=0)
    node_rank = lax.axis_index("wide") * lax.axis_size("narrow") + lax.axis_index("narrow")
    first_leaf = node_rank * leaves - NEAR_REACH
    local_index = near_index - first_leaf
    sources = extended[local_index]
    near_part = jnp.einsum("ljpq,ljpv->lqv", near_blocks, sources, precision=HIGH)
    return far_part + near_part


def solution(mesh):
    in_specs = (
        P(("wide", "narrow"), None, None),
        P(("wide", "narrow"), None, None),
        P(("wide", "narrow"), None, None),
        P(("wide", "narrow"), None, None),
        P(("wide", "narrow"), None, None),
        P(("wide", "narrow"), None, None, None),
        P("wide", "narrow", None, None),
        P(("wide", "narrow"), None, None),
        P(("wide", "narrow"), None, None),
        P(("wide", "narrow"), None, None, None),
        P(("wide", "narrow"), None),
        P(("wide", "narrow"), None),
        P("wide", "narrow"),
    )
    out_specs = P(("wide", "narrow"), None, None)
    return jax.shard_map(shards, mesh=mesh, in_specs=in_specs, out_specs=out_specs, check_vma=False)
```

profile of v0, /device:TPU:0, one launch (start us, length us, event | category | flops | bytes accessed | tf_op | source)
XLA Modules:
  0.0 259.9 jit_solution(13110974289088481287)
XLA Ops:
  6.5 0.0 copy-start
  6.5 0.0 copy-start.2
  6.5 0.0 copy-start.4
  6.5 0.0 all-reduce.3.cloned.1.call-start
  6.5 7.7 %fusion.14 = f32[12,128,256]{1,2,0:T(8,128)S(1)} fusion(f32[12,256,128]{2,1,0:T(8,128)} %param.14, f32[12,256,256]{2,1,0:T(8,128)} %param.13), kind=kOutput, calls=%fused_computation.26 | convolution fusion | flops 1207959552 | bytes 6291456 | tf_op jit(solution)/shard_map/lpk,lpv->lkv/dot_general | solution.py:34
  14.3 0.0 copy-done.2
  14.3 0.0 copy-start.7
  14.3 0.0 copy-start.8
  14.3 1.4 fusion.15
  15.7 0.0 copy-done.4
  15.7 0.0 copy-start.1
  15.7 0.9 convolution_bitcast_fusion.2
  16.6 0.0 all-reduce.3.cloned.1.call-update
  16.7 0.0 all-gather.6.cloned.1.call-start
  16.7 0.0 copy-done.1
  16.7 0.7 all-gather.6.cloned.1.call-update
  17.4 0.0 all-gather.4.cloned.1.call-start
  17.5 61.0 %all-reduce.3.cloned.1.call-done = f32[1,128,256]{1,2,0:T(8,128)} async-done(((f32[1,128,256]{1,2,0:T(8,128)}), f32[1,128,256]{1,2,0:T(8,128)}) %all-reduce.3.cloned.1.call-update) | async-done | bytes 131088 | tf_op jit(solution)/shard_map/psum | solution.py:38
  78.5 1.7 copy.25
  80.2 0.0 all-gather.4.cloned.1.call-update
  80.2 0.0 all-reduce.5.cloned.1.call-start
  80.2 2.1 fusion.13
  82.3 1.3 collective-permute-start
  83.7 1.5 collective-permute-start.1
  85.1 0.0 copy-done.7
  85.8 0.1 copy.26
  85.9 0.1 reshape.69
  86.0 0.0 copy-done.8
  86.0 0.0 collective-permute-done
  86.1 1.4 collective-permute-done.1
  87.5 4.3 %pad_maximum_fusion = f32[16,256,256]{2,1,0:T(8,128)} fusion(f32[2,256,256]{2,1,0:T(8,128)S(1)} %collective-permute-done.1, f32[12,256,256]{2,1,0:T(8,128)} %param.13, f32[2,256,256]{2,1,0:T(8,128)S(1)} %collective-permute-done), kind=kLoop, calls=%fused_computation.2 | loop fusion | flops 2097152 | bytes 8388608 | tf_op jit(solution)/shard_map/concatenate | solution.py:48
  91.7 0.0 copy-start.5
  91.7 10.0 %gather_fusion.1 = f32[48,256,256]{2,1,0:T(8,128)} fusion(f32[16,256,256]{2,1,0:T(8,128)} %pad_maximum_fusion, s32[1024]{0:T(1024)S(1)} %pad_clamp_fusion), kind=kCustom, calls=%fused_computation.1 | custom fusion | bytes 25166016 | tf_op jit(solution)/shard_map/gather | solution.py:52
  101.8 0.0 copy-start.3
  101.8 0.0 copy-start.6
  101.8 5.8 %all-gather.6.cloned.1.call-done = f32[1024,256]{0,1:T(8,128)} async-done(((f32[128,256]{0,1:T(8,128)}), f32[1024,256]{0,1:T(8,128)}) %all-gather.6.cloned.1.call-update) | async-done | bytes 1048592 | tf_op jit(solution)/shard_map/all_gather | solution.py:37
  107.6 1.6 copy.34
  109.2 0.6 gather_fusion
  109.7 45.5 %all-gather.4.cloned.1.call-done = f32[16,128,256]{2,1,0:T(8,128)} async-done(((f32[1,128,256]{2,1,0:T(8,128)}), f32[16,128,256]{2,1,0:T(8,128)}) %all-gather.4.cloned.1.call-update) | async-done | bytes 2097168 | tf_op jit(solution)/shard_map/all_gather | solution.py:41
  155.2 0.0 copy-done.5
  155.2 1.9 convolution_bitcast_fusion.1
  157.2 0.0 all-reduce.5.cloned.1.call-update
  157.2 0.0 copy-done.3
  157.2 0.6 convolution_bitcast_fusion
  157.8 58.3 %all-reduce.5.cloned.1.call-done = f32[128,256]{0,1:T(8,128)} async-done(((f32[128,256]{0,1:T(8,128)}), f32[128,256]{0,1:T(8,128)}) %all-reduce.5.cloned.1.call-update) | async-done | bytes 131088 | tf_op jit(solution)/shard_map/psum | solution.py:44
  216.1 0.0 copy-done.6
  216.1 1.2 fusion.3
  217.3 2.5 fusion.16
  219.9 0.0 copy-done
  219.9 2.9 %fusion.1 = f32[12,256,256]{2,1,0:T(8,128)S(1)} fusion(f32[12,256,128]{2,1,0:T(8,128)S(1)} %copy-done, f32[256,12,128]{2,0,1:T(8,128)S(1)} %fusion.16), kind=kOutput, calls=%fused_computation.5 | convolution fusion | flops 1207959552 | bytes 6291456 | tf_op jit(solution)/shard_map/lpk,lkv->lpv/dot_general | solution.py:47
  222.8 27.0 %fusion = f32[12,256,256]{1,2,0:T(8,128)} fusion(f32[12,256,256]{2,1,0:T(8,128)S(1)} %fusion.1, f32[12,4,256,256]{3,2,1,0:T(8,128)} %bitcast.62, f32[12,4,256,256]{3,2,1,0:T(8,128)} %param.22), kind=kOutput, calls=%fused_computation.4 | convolution fusion | flops 9664462848 | bytes 31457280 | tf_op jit(solution)/shard_map/ljpq,ljpv->lqv/dot_general | solution.py:53
  249.8 3.5 %copy.28 = f32[12,256,256]{2,1,0:T(8,128)} copy(f32[12,256,256]{1,2,0:T(8,128)} %fusion) | data formatting | bytes 6291456 | tf_op jit(solution)/shard_map/add | solution.py:54
  (4 shorter events, 0.0 us)
Async XLA Ops:
  6.5 213.3 %copy-start = (f32[12,256,128]{2,1,0:T(8,128)S(1)}, f32[12,256,128]{2,1,0:T(8,128)}, u32[]{:S(2)}) copy-start(f32[12,256,128]{2,1,0:T(8,128)} %param.15) | copy-start | bytes 4718596
  6.5 7.7 %copy-start.2 = (f32[12,128,128]{2,1,0:T(8,128)S(1)}, f32[12,128,128]{2,1,0:T(8,128)}, u32[]{:S(2)}) copy-start(f32[12,128,128]{2,1,0:T(8,128)} %param.16) | copy-start | bytes 2359300
  6.5 9.2 %copy-start.4 = (f32[1,128,128]{2,1,0:T(8,128)S(1)}, f32[1,128,128]{2,1,0:T(8,128)}, u32[]{:S(2)}) copy-start(f32[1,128,128]{2,1,0:T(8,128)} %param.17) | copy-start | bytes 196612
  6.5 72.0 %all-reduce.3.cloned.1.call-start = ((), (), s32[]{:S(2)}) async-start(), calls=%async_computation | async-start | bytes 262144 | tf_op jit(solution)/shard_map/psum | solution.py:38
  14.3 70.9 %copy-start.7 = (s32[12,4]{0,1:T(4,128)S(1)}, s32[12,4]{0,1:T(4,128)}, u32[]{:S(2)}) copy-start(s32[12,4]{0,1:T(4,128)} %param.23) | copy-start | bytes 580
  14.3 71.7 %copy-start.8 = (s32[1,2]{1,0:T(1,128)S(1)}, s32[1,2]{1,0:T(1,128)}, u32[]{:S(2)}) copy-start(s32[1,2]{1,0:T(1,128)} %param.24) | copy-start | bytes 28
  15.7 1.0 copy-start.1
  16.7 90.9 %all-gather.6.cloned.1.call-start = ((), (), s32[]{:S(2)}) async-start(), calls=%async_computation.3 | async-start | bytes 1179648 | tf_op jit(solution)/shard_map/all_gather | solution.py:37
  17.4 137.8 %all-gather.4.cloned.1.call-start = ((), (), s32[]{:S(2)}) async-start(), calls=%async_computation.1 | async-start | bytes 2228224 | tf_op jit(solution)/shard_map/all_gather | solution.py:41
  80.2 135.9 %all-reduce.5.cloned.1.call-start = ((), (), s32[]{:S(2)}) async-start(), calls=%async_computation.2 | async-start | bytes 262144 | tf_op jit(solution)/shard_map/psum | solution.py:44
  82.3 3.7 %collective-permute-start = (f32[2,256,256]{2,1,0:T(8,128)}, f32[2,256,256]{2,1,0:T(8,128)S(1)}, u32[]{:S(2)}, u32[]{:S(2)}) collective-permute-start(f32[2,256,256]{2,1,0:T(8,128)} %get-tuple-element.16), channel_id=1, source_target_pairs={{0,1},{1,2},{2,3},{3,4},{4,5},{5,6},{6,7},{7,8},{8,9},{9,10},{10,1... | collective-permute-start | bytes 1572872 | tf_op jit(solution)/shard_map/ppermute | solution.py:13
  83.7 3.8 %collective-permute-start.1 = (f32[2,256,256]{2,1,0:T(8,128)S(1)}, f32[2,256,256]{2,1,0:T(8,128)S(1)}, u32[]{:S(2)}, u32[]{:S(2)}) collective-permute-start(f32[2,256,256]{2,1,0:T(8,128)S(1)} %get-tuple-element.17), channel_id=1, source_target_pairs={{1,0},{2,1},{3,2},{4,3},{5,4},{6,5},{7,6},{8,7},{9,8},{10,9},{11,1... | collective-permute-start | bytes 1572872 | tf_op jit(solution)/shard_map/ppermute | solution.py:13
  91.7 63.5 %copy-start.5 = (f32[1,1,128,128]{3,2,1,0:T(8,128)S(1)}, f32[1,1,128,128]{3,2,1,0:T(8,128)}, u32[]{:S(2)}) copy-start(f32[1,1,128,128]{3,2,1,0:T(8,128)} %param.19) | copy-start | bytes 196612
  101.8 55.5 %copy-start.3 = (f32[1,2,128,128]{3,2,1,0:T(8,128)S(1)}, f32[1,2,128,128]{3,2,1,0:T(8,128)}, u32[]{:S(2)}) copy-start(f32[1,2,128,128]{3,2,1,0:T(8,128)} %param.18) | copy-start | bytes 393220
  101.8 114.4 %copy-start.6 = (f32[1,128,128]{2,1,0:T(8,128)S(1)}, f32[1,128,128]{2,1,0:T(8,128)}, u32[]{:S(2)}) copy-start(f32[1,128,128]{2,1,0:T(8,128)} %param.20) | copy-start | bytes 196612
Sparse Core Ops, SparseCore 0:
  16.8 61.6 all-reduce.2
  80.3 27.2 all-gather.5
  110.0 45.2 all-gather.3
  157.5 58.5 all-reduce.4
where the time goes:
time: 260 us
  waiting for transfers between devices  173 us (67%)
  matrix products  46.2 us (18%)
  local copies, waits for them, and re-layouts  19.7 us (8%)
  between operations  14 us (5%)
  other arithmetic  4.28 us (2%)
  starting transfers between devices  2.91 us (1%)
    psum x1, waiting for transfers between devices, shards(): group_coeffs = lax.psum(up_term, 'narrow')  61 us
    psum x1, waiting for transfers between devices, shards(): group_out = lax.psum(partial_value, 'narrow')  58.3 us
    all_gather x1, waiting for transfers between devices, shards(): all_groups = lax.all_gather(group_coeffs[None], 'wide', axis=0, tiled=True)  45.5 us
    dot_general x1, matrix products, shards(): jnp.einsum('ljpq,ljpv->lqv', near_blocks, sources, precision=HIGH)  27 us
    gather x1, local copies, waits for them, and re-layouts, shards(): sources = extended[local_index]  10 us
    dot_general x1, matrix products, shards(): jnp.einsum('lpk,lpv->lkv', row_basis, cotangent, precision=HIGH)  7.71 us
    all_gather x1, waiting for transfers between devices, shards(): siblings = lax.all_gather(node_coeffs[None], 'narrow', axis=0, tiled=True)  5.84 us
  transfers between devices with their start and end apart: 6, of which 5 were waited for; matrix products, arithmetic and copies ran while one was open for 8% of the time, Pallas kernels for 0%

commit v1 on v0

--- a/solution.py
+++ b/solution.py
@@ -35,7 +35,12 @@
     node_coeffs = jnp.einsum("lkm,lkv->mv", leaf_up, leaf_coeffs, precision=HIGH)
     up_term = jnp.dot(node_up[0].T, node_coeffs, precision=HIGH)
     siblings = lax.all_gather(node_coeffs[None], "narrow", axis=0, tiled=True)
-    group_coeffs = lax.psum(up_term, "narrow")
+    amount_of = lax.psum(1, "narrow")
+    group_coeffs = up_term
+    for jj in [it for it in (1, 2, 4, 8, 16) if it < amount_of]:
+        group_coeffs = group_coeffs + lax.ppermute(
+            group_coeffs, "narrow", tuple(((s, s ^ jj) for s in range(amount_of)))
+        )
     picked = siblings[far_nodes[0]]
     node_out = jnp.einsum("jkm,jkv->mv", node_couple[0], picked, precision=HIGH)
     all_groups = lax.all_gather(group_coeffs[None], "wide", axis=0, tiled=True)

time: 260 us -> 198 us (0.76)
  waiting for transfers between devices: 173 us -> 106 us
  starting transfers between devices: 2.91 us -> 8.04 us
    psum x1 -> x0, waiting for transfers between devices: 61 us -> none  [shards(): group_coeffs = lax.psum(up_term, 'narrow')]
    all_gather x1, waiting for transfers between devices: 45.5 us -> 36 us  [shards(): all_groups = lax.all_gather(group_coeffs[None], 'wide', axis=0, tiled=True)]
    ppermute x0 -> x3, waiting for transfers between devices: none -> 8.87 us  [shards(): lax.ppermute(group_coeffs, 'narrow', tuple(((s, s ^ jj) for s in range(am...]
    all_gather x1, waiting for transfers between devices: 5.84 us -> 0.01 us  [shards(): siblings = lax.all_gather(node_coeffs[None], 'narrow', axis=0, tiled=True)]
    ppermute x0 -> x3, starting transfers between devices: none -> 5.18 us  [shards(): lax.ppermute(group_coeffs, 'narrow', tuple(((s, s ^ jj) for s in range(am...]
  transfers between devices with their start and end apart: 6 -> 8, of which waited for: 5 -> 6; matrix products, arithmetic and copies ran while one was open for 8% -> 11% of each run, Pallas kernels for 0% -> 0%
where the time goes in v1:
time: 198 us
  waiting for transfers between devices  106 us (54%)
  matrix products  44.9 us (23%)
  local copies, waits for them, and re-layouts  20 us (10%)
  between operations  14 us (7%)
  starting transfers between devices  8.04 us (4%)
  other arithmetic  4.91 us (2%)
    psum x1, waiting for transfers between devices, shards(): group_out = lax.psum(partial_value, 'narrow')  58 us
    all_gather x1, waiting for transfers between devices, shards(): all_groups = lax.all_gather(group_coeffs[None], 'wide', axis=0, tiled=True)  36 us
    dot_general x1, matrix products, shards(): jnp.einsum('ljpq,ljpv->lqv', near_blocks, sources, precision=HIGH)  27 us
    gather x1, local copies, waits for them, and re-layouts, shards(): sources = extended[local_index]  9.9 us
    ppermute x3, waiting for transfers between devices, shards(): lax.ppermute(group_coeffs, 'narrow', tuple(((s, s ^ jj) for s in range(am...  8.87 us
    dot_general x1, matrix products, shards(): jnp.einsum('lpk,lpv->lkv', row_basis, cotangent, precision=HIGH)  7.71 us
    ppermute x3, starting transfers between devices, shards(): lax.ppermute(group_coeffs, 'narrow', tuple(((s, s ^ jj) for s in range(am...  5.18 us
    concatenate x1, other arithmetic, shards(): extended = jnp.concatenate([lower, cotangent, upper], axis=0)  4.2 us
  transfers between devices with their start and end apart: 8, of which 6 were waited for; matrix products, arithmetic and copies ran while one was open for 11% of the time, Pallas kernels for 0%

profile of v1, /device:TPU:0, one launch (start us, length us, event | category | flops | bytes accessed | tf_op | source)
XLA Modules:
  0.0 197.7 jit_solution(12663110009314069732)
XLA Ops:
  6.5 0.0 copy-start
  6.5 0.0 copy-start.1
  6.5 0.0 copy-start.4
  6.5 0.0 all-gather.5.cloned.1.call-start
  6.5 7.7 %fusion.11 = f32[12,128,256]{1,2,0:T(8,128)S(1)} fusion(f32[12,256,128]{2,1,0:T(8,128)} %param.14, f32[12,256,256]{2,1,0:T(8,128)} %param.13), kind=kOutput, calls=%fused_computation.24 | convolution fusion | flops 1207959552 | bytes 6291456 | tf_op jit(solution)/shard_map/lpk,lpv->lkv/dot_general | solution.py:34
  14.3 0.0 copy-done.1
  14.3 0.0 copy-start.7
  14.3 0.0 copy-start.8
  14.3 2.1 %fusion.12 = f32[256,128,1]{1,0,2:T(8,128)} fusion(f32[12,128,256]{1,2,0:T(8,128)S(1)} %fusion.11, f32[12,128,128]{2,1,0:T(8,128)S(1)} %copy-done.1), kind=kOutput, calls=%fused_computation.25 | convolution fusion | flops 603979776 | bytes 2490368 | tf_op jit(solution)/shard_map/lkm,lkv->mv/dot_general | solution.py:35
  16.3 0.0 all-gather.5.cloned.1.call-update
  16.4 0.0 all-gather.7.cloned.1.call-start
  16.4 0.0 copy-done.4
  16.4 1.2 convolution_bitcast_fusion.2
  17.6 0.1 collective-permute-start
  17.7 1.3 collective-permute-done
  19.0 1.7 collective-permute-start.1
  20.8 3.9 %collective-permute-done.1 = f32[128,256]{0,1:T(8,128)S(1)} collective-permute-done((f32[128,256]{0,1:T(8,128)S(1)}, f32[128,256]{0,1:T(8,128)S(1)}, u32[]{:S(2)}, u32[]{:S(2)}) %collective-permute-start.1) | collective-permute-done | bytes 131104 | tf_op jit(solution)/shard_map/ppermute | solution.py:41
  24.7 3.4 %collective-permute-start.2 = (f32[128,256]{0,1:T(8,128)S(1)}, f32[128,256]{0,1:T(8,128)S(1)}, u32[]{:S(2)}, u32[]{:S(2)}) collective-permute-start(f32[128,256]{0,1:T(8,128)S(1)} %add.46), channel_id=1, source_target_pairs={{0,4},{1,5},{2,6},{3,7},{4,0},{5,1},{6,2},{7,3},{8,12},{9,13},{10,... | collective-permute-start | bytes 393224 | tf_op jit(solution)/shard_map/ppermute | solution.py:41
  28.0 3.6 %collective-permute-done.2 = f32[128,256]{0,1:T(8,128)S(1)} collective-permute-done((f32[128,256]{0,1:T(8,128)S(1)}, f32[128,256]{0,1:T(8,128)S(1)}, u32[]{:S(2)}, u32[]{:S(2)}) %collective-permute-start.2) | collective-permute-done | bytes 131104 | tf_op jit(solution)/shard_map/ppermute | solution.py:41
  31.7 0.7 add.47
  32.4 0.0 all-gather.7.cloned.1.call-update
  32.4 0.0 all-reduce.2.cloned.1.call-start
  32.4 2.1 %fusion.10 = (f32[2,256,256]{2,1,0:T(8,128)}, f32[2,256,256]{2,1,0:T(8,128)S(1)}) fusion(f32[12,256,256]{2,1,0:T(8,128)} %param.13), kind=kLoop, calls=%fused_computation.23 | loop fusion | bytes 2097152 | tf_op jit(solution)/shard_map/slice | solution.py:32
  34.5 1.3 collective-permute-start.3
  35.8 1.5 collective-permute-start.4
  37.3 0.0 copy-done.7
  38.0 0.1 copy.18
  38.1 0.1 reshape.69
  38.2 0.0 copy-done.8
  38.2 0.0 collective-permute-done.3
  38.2 2.9 %collective-permute-done.4 = f32[2,256,256]{2,1,0:T(8,128)S(1)} collective-permute-done((f32[2,256,256]{2,1,0:T(8,128)S(1)}, f32[2,256,256]{2,1,0:T(8,128)S(1)}, u32[]{:S(2)}, u32[]{:S(2)}) %collective-permute-start.4) | collective-permute-done | bytes 524320 | tf_op jit(solution)/shard_map/ppermute | solution.py:13
  41.1 4.2 %pad_maximum_fusion = f32[16,256,256]{2,1,0:T(8,128)} fusion(f32[2,256,256]{2,1,0:T(8,128)S(1)} %collective-permute-done.4, f32[12,256,256]{2,1,0:T(8,128)} %param.13, f32[2,256,256]{2,1,0:T(8,128)S(1)} %collective-permute-done.3), kind=kLoop, calls=%fused_computation.2 | loop fusion | flops 2097152 | bytes 8388608 | tf_op jit(solution)/shard_map/concatenate | solution.py:53
  45.3 9.9 %gather_fusion.1 = f32[48,256,256]{2,1,0:T(8,128)} fusion(f32[16,256,256]{2,1,0:T(8,128)} %pad_maximum_fusion, s32[1024]{0:T(1024)S(1)} %pad_clamp_fusion), kind=kCustom, calls=%fused_computation.1 | custom fusion | bytes 25166016 | tf_op jit(solution)/shard_map/gather | solution.py:57
  55.2 0.0 copy-start.5
  55.2 0.0 all-gather.5.cloned.1.call-done
  55.2 1.6 copy.23
  56.8 0.0 copy-start.3
  56.8 0.0 copy-start.6
  56.8 0.6 gather_fusion
  57.4 0.0 copy-start.2
  57.4 36.0 %all-gather.7.cloned.1.call-done = f32[2048,256]{0,1:T(8,128)} async-done(((f32[128,256]{0,1:T(8,128)}), f32[2048,256]{0,1:T(8,128)}) %all-gather.7.cloned.1.call-update) | async-done | bytes 2097168 | tf_op jit(solution)/shard_map/all_gather | solution.py:46
  93.4 2.0 copy.24
  95.4 0.1 constant_dynamic-slice_fusion
  95.5 0.0 copy-done.5
  95.5 0.9 convolution_bitcast_fusion.1
  96.4 0.0 all-reduce.2.cloned.1.call-update
  96.4 0.0 copy-done.3
  96.4 0.6 convolution_bitcast_fusion
  97.0 58.0 %all-reduce.2.cloned.1.call-done = f32[128,256]{0,1:T(8,128)} async-done(((f32[128,256]{0,1:T(8,128)}), f32[128,256]{0,1:T(8,128)}) %all-reduce.2.cloned.1.call-update) | async-done | bytes 131088 | tf_op jit(solution)/shard_map/psum | solution.py:49
  155.1 0.0 copy-done.6
  155.1 1.2 fusion.3
  156.3 0.0 copy-done.2
  156.3 1.4 fusion.13
  157.7 0.0 copy-done
  157.7 2.9 %fusion.1 = f32[12,256,256]{2,1,0:T(8,128)S(1)} fusion(f32[12,256,128]{2,1,0:T(8,128)S(1)} %copy-done, f32[256,12,128]{2,0,1:T(8,128)S(1)} %fusion.13), kind=kOutput, calls=%fused_computation.5 | convolution fusion | flops 1207959552 | bytes 6291456 | tf_op jit(solution)/shard_map/lpk,lkv->lpv/dot_general | solution.py:52
  160.6 27.0 %fusion = f32[12,256,256]{1,2,0:T(8,128)} fusion(f32[12,256,256]{2,1,0:T(8,128)S(1)} %fusion.1, f32[12,4,256,256]{3,2,1,0:T(8,128)} %bitcast.63, f32[12,4,256,256]{3,2,1,0:T(8,128)} %param.22), kind=kOutput, calls=%fused_computation.4 | convolution fusion | flops 9664462848 | bytes 31457280 | tf_op jit(solution)/shard_map/ljpq,ljpv->lqv/dot_general | solution.py:58
  187.6 3.5 %copy.20 = f32[12,256,256]{2,1,0:T(8,128)} copy(f32[12,256,256]{1,2,0:T(8,128)} %fusion) | data formatting | bytes 6291456 | tf_op jit(solution)/shard_map/add | solution.py:59
  (6 shorter events, 0.1 us)
Async XLA Ops:
  6.5 151.1 %copy-start = (f32[12,256,128]{2,1,0:T(8,128)S(1)}, f32[12,256,128]{2,1,0:T(8,128)}, u32[]{:S(2)}) copy-start(f32[12,256,128]{2,1,0:T(8,128)} %param.15) | copy-start | bytes 4718596
  6.5 7.7 %copy-start.1 = (f32[12,128,128]{2,1,0:T(8,128)S(1)}, f32[12,128,128]{2,1,0:T(8,128)}, u32[]{:S(2)}) copy-start(f32[12,128,128]{2,1,0:T(8,128)} %param.16) | copy-start | bytes 2359300
  6.5 9.9 %copy-start.4 = (f32[1,128,128]{2,1,0:T(8,128)S(1)}, f32[1,128,128]{2,1,0:T(8,128)}, u32[]{:S(2)}) copy-start(f32[1,128,128]{2,1,0:T(8,128)} %param.17) | copy-start | bytes 196612
  6.5 48.7 %all-gather.5.cloned.1.call-start = ((), (), s32[]{:S(2)}) async-start(), calls=%async_computation.1 | async-start | bytes 1179648 | tf_op jit(solution)/shard_map/all_gather | solution.py:37
  14.3 23.1 %copy-start.7 = (s32[12,4]{0,1:T(4,128)S(1)}, s32[12,4]{0,1:T(4,128)}, u32[]{:S(2)}) copy-start(s32[12,4]{0,1:T(4,128)} %param.23) | copy-start | bytes 580
  14.3 23.9 %copy-start.8 = (s32[1,2]{1,0:T(1,128)S(1)}, s32[1,2]{1,0:T(1,128)}, u32[]{:S(2)}) copy-start(s32[1,2]{1,0:T(1,128)} %param.24) | copy-start | bytes 28
  16.4 77.0 %all-gather.7.cloned.1.call-start = ((), (), s32[]{:S(2)}) async-start(), calls=%async_computation.2 | async-start | bytes 2228224 | tf_op jit(solution)/shard_map/all_gather | solution.py:46
  17.6 1.4 collective-permute-start
  19.0 5.6 %collective-permute-start.1 = (f32[128,256]{0,1:T(8,128)S(1)}, f32[128,256]{0,1:T(8,128)S(1)}, u32[]{:S(2)}, u32[]{:S(2)}) collective-permute-start(f32[128,256]{0,1:T(8,128)S(1)} %add.45), channel_id=1, source_target_pairs={{0,2},{1,3},{2,0},{3,1},{4,6},{5,7},{6,4},{7,5},{8,10},{9,11},{10,... | collective-permute-start | bytes 393224 | tf_op jit(solution)/shard_map/ppermute | solution.py:41
  24.7 7.0 %collective-permute-start.2 = (f32[128,256]{0,1:T(8,128)S(1)}, f32[128,256]{0,1:T(8,128)S(1)}, u32[]{:S(2)}, u32[]{:S(2)}) collective-permute-start(f32[128,256]{0,1:T(8,128)S(1)} %add.46), channel_id=1, source_target_pairs={{0,4},{1,5},{2,6},{3,7},{4,0},{5,1},{6,2},{7,3},{8,12},{9,13},{10,... | collective-permute-start | bytes 393224 | tf_op jit(solution)/shard_map/ppermute | solution.py:41
  32.4 122.7 %all-reduce.2.cloned.1.call-start = ((), (), s32[]{:S(2)}) async-start(), calls=%async_computation | async-start | bytes 262144 | tf_op jit(solution)/shard_map/psum | solution.py:49
  34.5 3.7 %collective-permute-start.3 = (f32[2,256,256]{2,1,0:T(8,128)}, f32[2,256,256]{2,1,0:T(8,128)S(1)}, u32[]{:S(2)}, u32[]{:S(2)}) collective-permute-start(f32[2,256,256]{2,1,0:T(8,128)} %get-tuple-element.16), channel_id=1, source_target_pairs={{0,1},{1,2},{2,3},{3,4},{4,5},{5,6},{6,7},{7,8},{8,9},{9,10},{10,1... | collective-permute-start | bytes 1572872 | tf_op jit(solution)/shard_map/ppermute | solution.py:13
  35.8 5.3 %collective-permute-start.4 = (f32[2,256,256]{2,1,0:T(8,128)S(1)}, f32[2,256,256]{2,1,0:T(8,128)S(1)}, u32[]{:S(2)}, u32[]{:S(2)}) collective-permute-start(f32[2,256,256]{2,1,0:T(8,128)S(1)} %get-tuple-element.17), channel_id=1, source_target_pairs={{1,0},{2,1},{3,2},{4,3},{5,4},{6,5},{7,6},{8,7},{9,8},{10,9},{11,1... | collective-permute-start | bytes 1572872 | tf_op jit(solution)/shard_map/ppermute | solution.py:13
  55.2 40.3 %copy-start.5 = (f32[1,1,128,128]{3,2,1,0:T(8,128)S(1)}, f32[1,1,128,128]{3,2,1,0:T(8,128)}, u32[]{:S(2)}) copy-start(f32[1,1,128,128]{3,2,1,0:T(8,128)} %param.19) | copy-start | bytes 196612
  56.8 39.6 %copy-start.3 = (f32[1,2,128,128]{3,2,1,0:T(8,128)S(1)}, f32[1,2,128,128]{3,2,1,0:T(8,128)}, u32[]{:S(2)}) copy-start(f32[1,2,128,128]{3,2,1,0:T(8,128)} %param.18) | copy-start | bytes 393220
  56.8 98.2 %copy-start.6 = (f32[1,128,128]{2,1,0:T(8,128)S(1)}, f32[1,128,128]{2,1,0:T(8,128)}, u32[]{:S(2)}) copy-start(f32[1,128,128]{2,1,0:T(8,128)} %param.20) | copy-start | bytes 196612
  57.4 98.9 %copy-start.2 = (f32[12,128,128]{2,1,0:T(8,128)S(1)}, f32[12,128,128]{2,1,0:T(8,128)}, u32[]{:S(2)}) copy-start(f32[12,128,128]{2,1,0:T(8,128)} %param.21) | copy-start | bytes 2359300
Sparse Core Ops, SparseCore 0:
  16.5 27.1 all-gather.4
  45.8 47.5 all-gather.6
  96.5 58.4 all-reduce.1
